TPU v7x, 32 devices: a whole 2x2x4 slice. The times are simulated.
32 devices in a mesh: groups: 2 (over y), blk: 4 (over z), plane: 4 (over x, core).
Axes of the slice: x: 2, y: 2, z: 4, core: 2. Of those that a mesh axis runs over, the one named last changes fastest.
Arguments:
- orbitals: float32 [512, 1, 25600], P(('groups', 'blk'), None, 'plane'), parts along dimension 0, may hold values from -6 to 6
- kernel_half: float32 [1, 81, 81], replicated, may hold values from 0.1 to 10
- pair_own: int32 [384], P(('groups', 'blk')), parts along dimension 0, may hold values from 0 to 63
- pair_step: int32 [384], P(('groups', 'blk')), parts along dimension 0, may hold values from 0 to 2
- pair_remote: int32 [384], P(('groups', 'blk')), parts along dimension 0, may hold values from 0 to 63
- pair_count: int32 [8], P(('groups', 'blk')), parts along dimension 0, may hold values from 6 to 48, as said below
Outputs:
- exchange_part: float32 [512, 1, 25600], P(('groups', 'blk'), None, 'plane'), parts along dimension 0
There are 2 independent parts, one for each index of `groups`. A program takes and returns all parts, laid end to end along the dimension named above; an argument that names none is the same for every part. Nothing has to cross between parts.
Inputs may be any that keep to these rules, and one draw needn't show every extreme that they name: `pair_count`: slots at or beyond a block's count are ignored whatever they hold; in every draw some block has all 48 slots live.
All inputs are finite; a program needn't handle non-finite values.
Results may differ from a plain program's by a relative error of at most 0.0003.
Values sent between devices are 32-bit elements; how exact they have to be, the bound alone decides.
No kernel may reach another device: no remote copies, remote signals or barrier semaphores. Data moves between devices by JAX's collectives and lax.ppermute only.
A program may use at most 64 MiB of HBM per device.

v0:
```python
import jax
import jax.numpy as jnp
from jax import lax
from jax.sharding import PartitionSpec as P

NG = 160
STEPS = 3


highest = lax.Precision.HIGHEST


def from_behind(block, axis, distance):
    devices = range(lax.axis_size(axis))
    route = [((i - distance) % len(devices), i) for i in devices]
    return lax.ppermute(block, axis, route)


def cas_table(length):
    positions = jnp.arange(length, dtype=jnp.int32)
    product = positions[:, None] * positions[None, :] % length
    angles = 2.0 * jnp.pi / length * product.astype(jnp.float32)
    return jnp.cos(angles) + jnp.sin(angles)


def expand_kernel(kernel_half, length):
    positions = jnp.arange(length, dtype=jnp.int32)
    folded = jnp.minimum(positions, length - positions)
    columns = jnp.arange(kernel_half.shape[1], dtype=jnp.int32)
    picker = (folded[:, None] == columns[None, :]).astype(jnp.float32)
    halfway = jnp.einsum("ab,zbc->zac", picker, kernel_half, precision=highest)
    return jnp.einsum("zac,dc->zad", halfway, picker, precision=highest)


def local(orbitals, kernel_half, pair_own, pair_step, pair_remote, pair_count):
    planes = lax.axis_size("plane")
    block_rows, plane_depth, cell_count = orbitals.shape
    x_local = NG // planes
    cas_values = cas_table(NG)
    kernel = expand_kernel(kernel_half, NG)
    first_freq = lax.axis_index("plane") * x_local
    kernel_mine = jnp.transpose(lax.dynamic_slice_in_dim(kernel, first_freq, x_local, 2), (0, 2, 1))
    slot_count = pair_own.shape[0]
    remote = jnp.zeros((slot_count, plane_depth, cell_count), jnp.float32)
    visited = []
    carried = orbitals
    for offset in range(STEPS):
        carried = from_behind(carried, "blk", 1)
        visited.append(carried)
    for offset in range(STEPS):
        picked = jnp.take(visited[offset], pair_remote, axis=0)
        remote = jnp.where((pair_step == offset)[:, None, None], picked, remote)
    density = jnp.take(orbitals, pair_own, axis=0) * remote
    spectrum = jnp.einsum(
        "pzxy,yk->pzkx",
        density.reshape(slot_count, plane_depth, x_local, NG),
        cas_values,
        precision=highest,
    )
    spectrum = spectrum.reshape(slot_count, plane_depth, NG * x_local)
    cas_split = cas_values.reshape(planes, x_local, NG)
    columns = lax.all_to_all(spectrum, "plane", split_axis=2, concat_axis=1, tiled=True)
    item_count = columns.shape[0]
    pieces = columns.reshape(item_count, planes, plane_depth, x_local, x_local)
    frequency = (
        jnp.einsum("pszkx,sxq->pzkq", pieces, cas_split, precision=highest) * kernel_mine[None]
    )
    spatial = jnp.einsum("pzkq,sxq->pszkx", frequency, cas_split, precision=highest)
    spatial = spatial.reshape(item_count, planes * plane_depth, x_local * x_local)
    returned = lax.all_to_all(spatial, "plane", split_axis=1, concat_axis=2, tiled=True)
    returned = returned.reshape(slot_count, plane_depth, NG, x_local)
    potential = jnp.einsum("pzkx,ky->pzxy", returned, cas_values, precision=highest) / float(
        NG * NG
    )
    live_mask = (jnp.arange(slot_count, dtype=jnp.int32) < pair_count[0]).astype(jnp.float32)
    labels = jnp.arange(block_rows, dtype=jnp.int32)
    selector = (labels[:, None] == pair_own[None, :]).astype(jnp.float32) * live_mask[None, :]
    weighted = (potential.reshape(slot_count, plane_depth, cell_count) * remote).reshape(
        slot_count, plane_depth * cell_count
    )
    summed = jnp.dot(selector, weighted, precision=highest, preferred_element_type=jnp.float32)
    return summed.reshape(block_rows, plane_depth, cell_count)


def solution(mesh):
    in_specs = (
        P(("groups", "blk"), None, "plane"),
        P(),
        P(("groups", "blk")),
        P(("groups", "blk")),
        P(("groups", "blk")),
        P(("groups", "blk")),
    )
    out_specs = P(("groups", "blk"), None, "plane")
    return jax.shard_map(local, mesh=mesh, in_specs=in_specs, out_specs=out_specs, check_vma=False)
```

profile of v0, /device:TPU:9, one launch (start us, length us, event | category | flops | bytes accessed | tf_op | source)
XLA Modules:
  0.0 266.1 jit_solution(10861223638856836460)
XLA Ops:
  2.9 35.4 %collective-permute-done = f32[64,1,6400]{2,0,1:T(8,128)S(1)} collective-permute-done((f32[64,1,6400]{2,0,1:T(8,128)S(1)}, f32[64,1,6400]{2,0,1:T(8,128)S(1)}, u32[]{:S(2)}, u32[]{:S(2)}) %collective-permute-start) | collective-permute-done | bytes 1638432 | tf_op jit(solution)/shard_map/ppermute | solution.py:16
  39.6 36.0 %collective-permute-done.1 = f32[64,1,6400]{2,0,1:T(8,128)} collective-permute-done((f32[64,1,6400]{2,0,1:T(8,128)S(1)}, f32[64,1,6400]{2,0,1:T(8,128)}, u32[]{:S(2)}, u32[]{:S(2)}) %collective-permute-start.1) | collective-permute-done | bytes 1638432 | tf_op jit(solution)/shard_map/ppermute | solution.py:16
  77.7 2.0 gather_fusion.3
  79.7 3.9 %gather_fusion.2 = f32[48,6400]{1,0:T(8,128)} fusion(f32[64,6400]{1,0:T(8,128)} %bitcast.7, s32[1024]{0:T(1024)S(1)} %pad_clamp_fusion), kind=kCustom, calls=%fused_computation.2.clone | custom fusion | bytes 2457792 | tf_op jit(solution)/shard_map/jit(_take)/gather | solution.py:51
  83.6 29.3 %collective-permute-done.2 = f32[64,1,6400]{2,0,1:T(8,128)} collective-permute-done((f32[64,1,6400]{2,0,1:T(8,128)}, f32[64,1,6400]{2,0,1:T(8,128)}, u32[]{:S(2)}, u32[]{:S(2)}) %collective-permute-start.2) | collective-permute-done | bytes 1638432 | tf_op jit(solution)/shard_map/ppermute | solution.py:16
  112.9 4.0 %gather_fusion.1 = f32[48,6400]{1,0:T(8,128)} fusion(f32[64,6400]{1,0:T(8,128)} %bitcast.5, s32[1024]{0:T(1024)S(1)} %pad_clamp_fusion), kind=kCustom, calls=%fused_computation.1.clone | custom fusion | bytes 2457792 | tf_op jit(solution)/shard_map/jit(_take)/gather | solution.py:51
  116.9 3.7 %fusion.12 = (f32[48,1,6400]{2,0,1:T(8,128)S(1)}, f32[48,1,6400]{2,0,1:T(8,128)}) fusion(f32[48,6400]{1,0:T(8,128)S(1)} %copy-done, pred[48]{0:T(512)(128)(4,1)S(1)} %get-tuple-element.14, f32[48,6400]{1,0:T(8,128)} %gather_fusion.3, pred[48]{0:T(512)(128)(4,1)S(1)} %get-tuple-element.11, f32[48,6400]{1,0:T(8,128)} %gather_fusion.2, ...), kind=kLoop, calls=%fused_computation.20 | loop fusion | flops 2457600 | bytes 7373040 | tf_op jit(solution)/shard_map/mul | solution.py:53
  121.7 4.0 %fusion.5 = f32[48,1,160,40]{2,0,3,1:T(8,128)} fusion(f32[48,40,160]{2,1,0:T(8,128)S(1)} %reshape.169), kind=kOutput, calls=%fused_computation.10 | convolution fusion | flops 590080000 | bytes 2457600 | tf_op jit(solution)/shard_map/pzxy,yk->pzkx/dot_general | solution.py:54
  125.7 3.0 %copy.29 = f32[48,1,160,40]{0,3,2,1:T(8,128)S(1)} copy(f32[48,1,160,40]{2,0,3,1:T(8,128)} %fusion.5) | data formatting | bytes 2457600 | tf_op jit(solution)/shard_map/reshape | solution.py:60
  129.2 30.8 %reduce = f32[6400,48]{1,0:T(8,128)} reduce(f32[6400,1,48]{2,1,0:T(1,128)S(1)} %bitcast.93, f32[]{:T(128)} %broadcast.166), dimensions={1}, to_apply=%bitcast.80.reduce_sub_computation | reduce | bytes 2457604
  160.0 5.5 %reshape.243 = f32[4,1,76800]{2,1,0:T(1,128)} reshape(f32[6400,48]{1,0:T(8,128)} %reduce) | data formatting | bytes 2457600
  165.5 6.7 %all-to-all-start = ((f32[4,1,76800]{2,1,0:T(1,128)}), f32[4,1,76800]{2,1,0:T(1,128)S(1)}, u32[]{:S(2)}, u32[]{:S(2)}) async-start(f32[4,1,76800]{2,1,0:T(1,128)} %reshape.243), calls=%async_computation | async-start | bytes 2457600 | tf_op jit(solution)/shard_map/all_to_all | solution.py:62
  172.9 14.6 %all-to-all-done = f32[4,1,76800]{2,1,0:T(1,128)S(1)} async-done(((f32[4,1,76800]{2,1,0:T(1,128)}), f32[4,1,76800]{2,1,0:T(1,128)S(1)}, u32[]{:S(2)}, u32[]{:S(2)}) %all-to-all-start) | async-done | bytes 1228832 | tf_op jit(solution)/shard_map/all_to_all | solution.py:62
  187.5 5.3 %reduce.1 = f32[4,76800]{1,0:T(4,128)} reduce(f32[4,1,76800]{2,1,0:T(1,128)S(1)} %all-to-all-done, f32[]{:T(128)} %broadcast.166), dimensions={1}, to_apply=%all_to_all.4.reduce_sub_computation | reduce | bytes 2457604 | tf_op jit(solution)/shard_map/all_to_all | solution.py:62
  192.7 8.2 %reshape.244 = f32[6400,1,48]{2,1,0:T(1,128)S(1)} reshape(f32[4,76800]{1,0:T(4,128)} %reduce.1) | data formatting | bytes 2457600
  201.0 19.2 %fusion.21 = f32[48,40,160,1]{2,0,1,3:T(8,128)S(1)} fusion(f32[48,4,40,40]{0,3,2,1:T(8,128)S(1)} %bitcast.92, s32[4,40]{1,0:T(4,128)S(1)} %multiply_add_fusion), kind=kOutput, calls=%fused_computation.32 | convolution fusion | flops 590080000 | bytes 2458240 | tf_op jit(solution)/shard_map/pszkx,sxq->pzkq/dot_general | solution.py:66
  220.2 3.8 %fusion.1 = f32[4,40,48,40]{2,1,3,0:T(8,128)S(1)} fusion(f32[48,40,160,1]{2,0,1,3:T(8,128)S(1)} %fusion.21, f32[40,160]{1,0:T(8,128)S(1)} %dynamic-slice_bitcast_fusion, s32[4,40]{1,0:T(4,128)S(1)} %multiply_add_fusion), kind=kOutput, calls=%fused_computation.7 | convolution fusion | flops 590387200 | bytes 2483840 | tf_op jit(solution)/shard_map/pzkq,sxq->pszkx/dot_general | solution.py:68
  224.0 2.0 copy.22
  226.0 4.4 %all-to-all-start.1 = ((f32[48,4,1600]{2,0,1:T(8,128)}), f32[48,4,1600]{2,0,1:T(8,128)S(1)}, u32[]{:S(2)}, u32[]{:S(2)}) async-start(f32[48,4,1600]{2,0,1:T(8,128)} %copy.22), calls=%async_computation.1 | async-start | bytes 2555904 | tf_op jit(solution)/shard_map/all_to_all | solution.py:70
  231.1 15.4 %all-to-all-done.1 = f32[48,4,1600]{2,0,1:T(8,128)S(1)} async-done(((f32[48,4,1600]{2,0,1:T(8,128)}), f32[48,4,1600]{2,0,1:T(8,128)S(1)}, u32[]{:S(2)}, u32[]{:S(2)}) %all-to-all-start.1) | async-done | bytes 1228832 | tf_op jit(solution)/shard_map/all_to_all | solution.py:70
  247.0 3.2 %reshape.174 = f32[48,160,40]{2,1,0:T(8,128)} reshape(f32[48,4,1600]{2,1,0:T(4,128)S(1)} %copy.23) | data formatting | bytes 2457600 | tf_op jit(solution)/shard_map/reshape.31
  250.2 9.2 %convolution_multiply_fusion = f32[48,40,160]{2,1,0:T(8,128)S(1)} fusion(f32[48,160,40]{2,1,0:T(8,128)} %reshape.174), kind=kOutput, calls=%fused_computation.11 | convolution fusion | flops 590387200 | bytes 2457600 | tf_op jit(solution)/shard_map/pzkx,ky->pzxy/dot_general | solution.py:72
  260.4 2.7 %convolution_bitcast_fusion = f32[64,1,6400]{2,0,1:T(8,128)S(1)} fusion(f32[48,1,6400]{2,0,1:T(8,128)S(1)} %reshape.175, f32[48,1,6400]{2,0,1:T(8,128)} %get-tuple-element.7, f32[48]{0:T(128)S(1)} %compare_convert_fusion, s32[48]{0:T(128)S(1)} %copy-done.2), kind=kOutput, calls=%fused_computation.4 | convolution fusion | flops 236242944 | bytes 4096384 | tf_op jit(solution)/shard_map/dot_general | solution.py:81
  263.1 2.8 %copy.25 = f32[64,1,6400]{2,1,0:T(1,128)} copy(f32[64,1,6400]{2,0,1:T(8,128)S(1)} %convolution_bitcast_fusion) | data formatting | bytes 3276800 | tf_op jit(solution)/shard_map/reshape | solution.py:82
  (31 shorter events, 9.9 us)
Async XLA Ops:
  0.0 75.6 %copy-start.2 = (s32[48]{0:T(128)S(1)}, s32[48]{0:T(128)}, u32[]{:S(2)}) copy-start(s32[48]{0:T(128)} %param.10) | copy-start | bytes 580
  1.6 36.7 %collective-permute-start = (f32[64,1,6400]{2,0,1:T(8,128)S(1)}, f32[64,1,6400]{2,0,1:T(8,128)S(1)}, u32[]{:S(2)}, u32[]{:S(2)}) collective-permute-start(f32[64,1,6400]{2,0,1:T(8,128)S(1)} %copy.45), channel_id=1, source_target_pairs={{12,0},{0,4},{4,8},{8,12},{13,1},{1,5},{5,9},{9,13},{14,2},{2,6},{... | collective-permute-start | bytes 4915208 | tf_op jit(solution)/shard_map/ppermute | solution.py:16
  38.3 37.3 %collective-permute-start.1 = (f32[64,1,6400]{2,0,1:T(8,128)S(1)}, f32[64,1,6400]{2,0,1:T(8,128)}, u32[]{:S(2)}, u32[]{:S(2)}) collective-permute-start(f32[64,1,6400]{2,0,1:T(8,128)S(1)} %collective-permute-done), channel_id=1, source_target_pairs={{12,0},{0,4},{4,8},{8,12},{13,1},{1,5},{5,9},{9,13},{14,2},{2,6},{... | collective-permute-start | bytes 4915208 | tf_op jit(solution)/shard_map/ppermute | solution.py:16
  75.6 37.2 %collective-permute-start.2 = (f32[64,1,6400]{2,0,1:T(8,128)}, f32[64,1,6400]{2,0,1:T(8,128)}, u32[]{:S(2)}, u32[]{:S(2)}) collective-permute-start(f32[64,1,6400]{2,0,1:T(8,128)} %collective-permute-done.1), channel_id=1, source_target_pairs={{12,0},{0,4},{4,8},{8,12},{13,1},{1,5},{5,9},{9,13},{14,2},{2,6},{... | collective-permute-start | bytes 4915208 | tf_op jit(solution)/shard_map/ppermute | solution.py:16
  75.6 2.0 copy-start.3
  75.7 2.0 copy-start.4
  112.9 4.0 %copy-start = (f32[48,6400]{1,0:T(8,128)S(1)}, f32[48,6400]{1,0:T(8,128)}, u32[]{:S(2)}) copy-start(f32[48,6400]{1,0:T(8,128)} %gather_fusion) | copy-start | bytes 3686404
  165.5 6.8 %copy-start.1 = (f32[1,81,81]{2,0,1:T(1,128)S(1)}, f32[1,81,81]{2,0,1:T(1,128)}, u32[]{:S(2)}) copy-start(f32[1,81,81]{2,0,1:T(1,128)} %param.9) | copy-start | bytes 78736
  165.5 22.0 %all-to-all-start = ((f32[4,1,76800]{2,1,0:T(1,128)}), f32[4,1,76800]{2,1,0:T(1,128)S(1)}, u32[]{:S(2)}, u32[]{:S(2)}) async-start(f32[4,1,76800]{2,1,0:T(1,128)} %reshape.243), calls=%async_computation | async-start | bytes 2457600 | tf_op jit(solution)/shard_map/all_to_all | solution.py:62
  226.0 20.4 %all-to-all-start.1 = ((f32[48,4,1600]{2,0,1:T(8,128)}), f32[48,4,1600]{2,0,1:T(8,128)S(1)}, u32[]{:S(2)}, u32[]{:S(2)}) async-start(f32[48,4,1600]{2,0,1:T(8,128)} %copy.22), calls=%async_computation.1 | async-start | bytes 2555904 | tf_op jit(solution)/shard_map/all_to_all | solution.py:70
where the time goes:
time: 271 us; the launch traced here: 266 us
  waiting for transfers between devices  131 us (48%)
  local copies, waits for them, and re-layouts  41.4 us (15%)
  other arithmetic  39.8 us (15%)
  matrix products  39.5 us (15%)
  starting transfers between devices  13.7 us (5%)
    ppermute x3, waiting for transfers between devices, from_behind(): return lax.ppermute(block, axis, route)  101 us
    unnamed x1, other arithmetic  30.8 us
    dot_general x1, matrix products, local(): jnp.einsum('pszkx,sxq->pzkq', pieces, cas_split, precision=highest)  19.2 us
    unnamed x14, local copies, waits for them, and re-layouts  15.9 us
    all_to_all x1, waiting for transfers between devices, local(): lax.all_to_all(spatial, 'plane', split_axis=1, concat_axis=2, tiled=True)  15.4 us
    all_to_all x1, waiting for transfers between devices, local(): lax.all_to_all(spectrum, 'plane', split_axis=2, concat_axis=1, tiled=True)  14.6 us
    gather x3, local copies, waits for them, and re-layouts, local(): picked = jnp.take(visited[offset], pair_remote, axis=0)  9.92 us
    dot_general x1, matrix products, local(): jnp.einsum('pzkx,ky->pzxy', returned, cas_values, precision=highest)  9.23 us
  transfers between devices with their start and end apart: 5, of which 5 were waited for; matrix products, arithmetic and copies ran while one was open for 3% of the time, Pallas kernels for 0%

commit v1 on v0

v1 whole, which is shorter than its diff:
```python
import functools

import jax
import jax.numpy as jnp
import ml_dtypes
import numpy as np
from jax import lax
from jax.experimental import pallas as pl
from jax.experimental.pallas import tpu as pltpu
from jax.sharding import PartitionSpec as P

NG = 160
STEPS = 3
LANES = 128
GROUP = 4
LINES = 5
CAPACITIES = (16, 20, 24)

VMEM_LIMIT = 48 * 1024 * 1024
smem = pl.BlockSpec(memory_space=pltpu.SMEM)
vmem = pl.BlockSpec(memory_space=pltpu.VMEM)
hbm = pl.BlockSpec(memory_space=pl.ANY)


def split_table(table):
    high = table.astype(ml_dtypes.bfloat16)
    low = (table - high.astype(np.float64)).astype(ml_dtypes.bfloat16)
    return high, low


def make_tables(x_local):
    positions = np.arange(NG)
    angles = 2.0 * np.pi / NG * (positions[:, None] * positions[None, :] % NG)
    cas = np.cos(angles) + np.sin(angles)
    into = np.zeros((GROUP, 2 * LANES, NG))
    for r in range(GROUP):
        start = r * NG - r * LANES
        into[r, start : start + NG] = cas
    back = np.transpose(into, (0, 2, 1)).copy()
    order = np.arange(NG).reshape(NG // GROUP, GROUP).T.reshape(-1)
    mixed = cas[:, order]
    return split_table(into), split_table(back), split_table(mixed), split_table(mixed.T.copy())


def split_value(value):
    high = value.astype(jnp.bfloat16)
    low = (value - high.astype(jnp.float32)).astype(jnp.bfloat16)
    return high, low


def dot(a, b):
    return lax.dot_general(a, b, (((1,), (0,)), ((), ())), preferred_element_type=jnp.float32)


def dot3(a, b):
    return dot(a[0], b[0]) + (dot(a[0], b[1]) + dot(a[1], b[0]))


def plan_kernel(slots, orbs, planes, own, step, remote, count, request, place, seen, known):
    for s in range(STEPS):
        for k in range(slots):
            request[s * slots + k] = 0
        request[STEPS * slots + s] = 0
        for k in range(orbs):
            seen[s * orbs + k] = -1

    def visit(j, carry):
        live = j < count[0]
        s = jnp.where(live, step[j], 0)
        k = remote[j]
        at = seen[s * orbs + k]
        used = request[STEPS * slots + s]

        @pl.when(live & (at < 0))
        def _():
            request[s * slots + used] = k
            seen[s * orbs + k] = used
            request[STEPS * slots + s] = used + 1

        known[j] = jnp.where(live, s, 0)
        known[slots + j] = jnp.where(live, jnp.where(at < 0, used, at), 0)
        known[2 * slots + j] = jnp.where(live, own[j], -1)
        return carry

    lax.fori_loop(0, slots, visit, 0)
    me = lax.axis_index("plane")
    each = slots // planes
    for k in range(planes):
        first = partner(me, k, planes) * each
        for q in range(each):
            for part in range(3):
                place[part * slots + k * each + q] = known[part * slots + first + q]


def pack_kernel(capacity, slots, lines, wanted, orbitals, *sends):
    for s in range(STEPS):
        for c in range(capacity):
            row = wanted[s, c]
            sends[s][pl.ds(c * lines, lines), :] = orbitals[pl.ds(row * lines, lines), :]


def fetch(received, held, sems, size):
    copies = [
        pltpu.make_async_copy(received[s], held.at[pl.ds(s * size, size), :], sems.at[s])
        for s in range(STEPS)
    ]
    for copy in copies:
        copy.start()
    for copy in copies:
        copy.wait()


def density_kernel(capacity, slots, lines, planes, place, orbitals, *refs):
    received, parts, (held, sems) = refs[:STEPS], refs[STEPS : STEPS + planes], refs[STEPS + planes :]
    fetch(received, held, sems, capacity * lines)
    each = slots // planes
    for j in range(slots):
        far = (place[j] * capacity + place[slots + j]) * lines
        near = jnp.maximum(place[2 * slots + j], 0) * lines
        parts[j // each][pl.ds(j % each * lines, lines), :] = (
            orbitals[pl.ds(near, lines), :] * held[pl.ds(far, lines), :]
        )


def sum_kernel(capacity, slots, lines, planes, place, *refs):
    received, parts = refs[:STEPS], refs[STEPS : STEPS + planes]
    out, held, sems = refs[STEPS + planes :]
    copies = [
        pltpu.make_async_copy(
            received[s],
            held.at[pl.ds(s * capacity * lines, capacity * lines), :],
            sems.at[s],
        )
        for s in range(STEPS)
    ]
    for copy in copies:
        copy.start()
    out[...] = jnp.zeros_like(out)
    for copy in copies:
        copy.wait()
    each = slots // planes
    for j in range(slots):
        far = (place[j] * capacity + place[slots + j]) * lines
        near = place[2 * slots + j] * lines

        @pl.when(near >= 0)
        def _():
            out[pl.ds(near, lines), :] += (
                parts[j // each][pl.ds(j % each * lines, lines), :] * held[pl.ds(far, lines), :]
            )


def transform_kernel(pairs, lines, planes, *refs):
    parts = refs[:planes]
    into_hi, into_lo, back_hi, back_lo, mix_hi, mix_lo, unmix_hi, unmix_lo, kernel = refs[
        planes : planes + 9
    ]
    outs = refs[planes + 9 : 2 * planes + 9]
    cells, waves, result = refs[2 * planes + 9 :]
    whole = planes * lines
    rows = NG // GROUP
    me = lax.axis_index("plane")
    for k in range(planes):
        slab = partner(me, k, planes) * lines
        for p in range(pairs):
            cells[pl.ds(p * whole + slab, lines), :] = parts[k][pl.ds(p * lines, lines), :]
    line = [split_value(cells[pl.ds(t, pairs * rows, stride=LINES), :]) for t in range(LINES)]
    for r in range(GROUP):
        wide = [jnp.concatenate([line[r][i], line[r + 1][i]], axis=1) for i in range(2)]
        found = dot3(wide, (into_hi[r], into_lo[r]))
        for p in range(pairs):
            waves[p, r * rows : (r + 1) * rows, :] = found[p * rows : (p + 1) * rows, :]
    mix = (mix_hi[...], mix_lo[...])
    unmix = (unmix_hi[...], unmix_lo[...])
    for p in range(pairs):
        spectrum = dot3(mix, split_value(waves[p])) * kernel[...]
        waves[p] = dot3(unmix, split_value(spectrum))
    carried = None
    for r in range(GROUP):
        mine = jnp.concatenate(
            [waves[p, r * rows : (r + 1) * rows, :] for p in range(pairs)], axis=0
        )
        wide = dot3(split_value(mine), (back_hi[r], back_lo[r]))
        first = wide[:, :LANES] if carried is None else wide[:, :LANES] + carried
        carried = wide[:, LANES:]
        result[pl.ds(r, pairs * rows, stride=LINES), :] = first
    result[pl.ds(GROUP, pairs * rows, stride=LINES), :] = carried
    for k in range(planes):
        slab = partner(me, k, planes) * lines
        for p in range(pairs):
            outs[k][pl.ds(p * lines, lines), :] = result[pl.ds(p * whole + slab, lines), :]


def params():
    return pltpu.CompilerParams(vmem_limit_bytes=VMEM_LIMIT)


def floats(rows):
    return jax.ShapeDtypeStruct((rows, LANES), jnp.float32)


def partner(i, k, size):
    return i ^ k if size & (size - 1) == 0 else (k - i) % size


def exchange(parts, size):
    return [parts[0] if size & (size - 1) == 0 else lax.ppermute(parts[0], "plane", pairs_of(0, size))] + [
        lax.ppermute(parts[k], "plane", pairs_of(k, size)) for k in range(1, size)
    ]


def pairs_of(k, size):
    return [(i, partner(i, k, size)) for i in range(size)]


def local(orbitals, kernel_half, pair_own, pair_step, pair_remote, pair_count):
    planes = lax.axis_size("plane")
    blocks = lax.axis_size("blk")
    orbs, depth, cell_count = orbitals.shape
    slots = pair_own.shape[0]
    lines = cell_count // LANES
    each = slots // planes
    x_local = NG // planes
    flat = orbitals.reshape(orbs * lines, LANES)

    request, place = pl.pallas_call(
        functools.partial(plan_kernel, slots, orbs, planes),
        out_shape=(
            jax.ShapeDtypeStruct((STEPS * slots + STEPS,), jnp.int32),
            jax.ShapeDtypeStruct((3 * slots,), jnp.int32),
        ),
        in_specs=[smem] * 4,
        out_specs=(smem, smem),
        scratch_shapes=[
            pltpu.SMEM((STEPS * orbs,), jnp.int32),
            pltpu.SMEM((3 * slots,), jnp.int32),
        ],
        name="plan",
    )(pair_own, pair_step, pair_remote, pair_count)

    everyone = lax.all_gather(request, ("groups", "blk"))
    largest = jnp.max(everyone[:, STEPS * slots :])
    group = lax.axis_index("groups")
    block = lax.axis_index("blk")
    wanted = jnp.stack(
        [
            lax.dynamic_slice(
                everyone,
                (group * blocks + (block + s + 1) % blocks, s * slots),
                (1, slots),
            )[0]
            for s in range(STEPS)
        ]
    )

    half = kernel_half[0]
    tall = jnp.concatenate([half, half[1 : NG // 2][::-1]], axis=0)
    kernel = jnp.concatenate([tall, tall[:, 1 : NG // 2][:, ::-1]], axis=1) / float(NG * NG)
    tables = [jnp.asarray(part) for pair in make_tables(x_local) for part in pair]

    def run(capacity, flat, wanted, place, kernel, *tables):
        sends = pl.pallas_call(
            functools.partial(pack_kernel, capacity, slots, lines),
            out_shape=[floats(capacity * lines)] * STEPS,
            in_specs=[smem, vmem],
            out_specs=[vmem] * STEPS,
            compiler_params=params(),
            name="pack",
        )(wanted, flat)
        received = [
            lax.ppermute(
                sends[s], "blk", [(i, (i + s + 1) % blocks) for i in range(blocks)]
            )
            for s in range(STEPS)
        ]
        held = [
            pltpu.VMEM((STEPS * capacity * lines, LANES), jnp.float32),
            pltpu.SemaphoreType.DMA((STEPS,)),
        ]
        parts = pl.pallas_call(
            functools.partial(density_kernel, capacity, slots, lines, planes),
            out_shape=[floats(each * lines)] * planes,
            in_specs=[smem, vmem] + [hbm] * STEPS,
            out_specs=[vmem] * planes,
            scratch_shapes=held,
            compiler_params=params(),
            name="density",
        )(place, flat, *received)
        columns = exchange(parts, planes)
        backs = pl.pallas_call(
            functools.partial(transform_kernel, each, lines, planes),
            out_shape=[floats(each * lines)] * planes,
            in_specs=[vmem] * (planes + 9),
            out_specs=[vmem] * planes,
            scratch_shapes=[
                pltpu.VMEM((each * planes * lines, LANES), jnp.float32),
                pltpu.VMEM((each, NG, NG), jnp.float32),
                pltpu.VMEM((each * planes * lines, LANES), jnp.float32),
            ],
            compiler_params=params(),
            name="transform",
        )(*columns, *tables, kernel)
        potentials = exchange(backs, planes)
        return pl.pallas_call(
            functools.partial(sum_kernel, capacity, slots, lines, planes),
            out_shape=floats(orbs * lines),
            in_specs=[smem] + [hbm] * STEPS + [vmem] * planes,
            out_specs=vmem,
            scratch_shapes=held,
            compiler_params=params(),
            name="sum",
        )(place, *received, *potentials)

    sizes = [c for c in CAPACITIES if c < slots] + [slots]
    choice = sum((largest > c).astype(jnp.int32) for c in sizes[:-1])
    summed = lax.switch(
        choice,
        [functools.partial(run, c) for c in sizes],
        flat,
        wanted,
        place,
        kernel,
        *tables,
    )
    return summed.reshape(orbs, depth, cell_count)


def solution(mesh):
    in_specs = (
        P(("groups", "blk"), None, "plane"),
        P(),
        P(("groups", "blk")),
        P(("groups", "blk")),
        P(("groups", "blk")),
        P(("groups", "blk")),
    )
    out_specs = P(("groups", "blk"), None, "plane")
    return jax.shard_map(local, mesh=mesh, in_specs=in_specs, out_specs=out_specs, check_vma=False)
```

time: 271 us -> 110 us (0.41); the launches traced: 266 us -> 110 us
  waiting for transfers between devices: 131 us -> 72.6 us
  matrix products: 39.5 us -> 0 us
  other arithmetic: 39.8 us -> 0.92 us
  local copies, waits for them, and re-layouts: 41.4 us -> 5.39 us
  Pallas kernels: 0 us -> 11.7 us
  blocking collectives: 0 us -> 8.9 us
  starting transfers between devices: 13.7 us -> 6.71 us
    dot_general x7 -> x0, matrix products: 39.5 us -> none  [the longest x1 19.2 us: local(): jnp.einsum('pszkx,sxq->pzkq', pieces, cas_split, precision=highest)]
    unnamed x1 -> x0, other arithmetic: 30.8 us -> none
    all_to_all x2 -> x0, waiting for transfers between devices: 30 us -> none  [the longest x1 15.4 us: local(): lax.all_to_all(spatial, 'plane', split_axis=1, concat_axis=2, tiled=True)]
    ppermute x3 -> x9, waiting for transfers between devices: 101 us -> 72.6 us  [the longest x3 45.1 us: run(): lax.ppermute(sends[s], 'blk', [(i, (i + s + 1) % blocks) for i in range(b...]
    gather x4 -> x0, local copies, waits for them, and re-layouts: 11.9 us -> none  [the longest x3 9.92 us: local(): picked = jnp.take(visited[offset], pair_remote, axis=0)]
    unnamed x14 -> x7, local copies, waits for them, and re-layouts: 15.9 us -> 4.09 us
    pallas_call x0 -> x5, Pallas kernels: none -> 11.7 us  [the longest x1 3.71 us: run(): pl.pallas_call(functools.partial(transform_kernel, each, lines, planes),...]
    all_to_all x2 -> x0, starting transfers between devices: 11.1 us -> none  [the longest x1 6.72 us: local(): lax.all_to_all(spectrum, 'plane', split_axis=2, concat_axis=1, tiled=True)]
  transfers between devices with their start and end apart: 5 -> 9, of which waited for: 5 -> 7; matrix products, arithmetic and copies ran while one was open for 3% -> 0% of each run, Pallas kernels for 0% -> 0%
where the time goes in v1:
time: 110 us
  waiting for transfers between devices  72.6 us (66%)
  Pallas kernels  11.7 us (11%)
  blocking collectives  8.9 us (8%)
  starting transfers between devices  6.71 us (6%)
  local copies, waits for them, and re-layouts  5.39 us (5%)
  between operations  3.32 us (3%)
    ppermute x3, waiting for transfers between devices, run(): lax.ppermute(sends[s], 'blk', [(i, (i + s + 1) % blocks) for i in range(b...  45.1 us
    ppermute x6, waiting for transfers between devices, exchange(): lax.ppermute(parts[k], 'plane', pairs_of(k, size))  27.5 us
    unnamed x1, blocking collectives  8.9 us
    ppermute x6, starting transfers between devices, exchange(): lax.ppermute(parts[k], 'plane', pairs_of(k, size))  4.48 us
    unnamed x7, local copies, waits for them, and re-layouts  4.09 us
    pallas_call x1, Pallas kernels, run(): pl.pallas_call(functools.partial(transform_kernel, each, lines, planes),...  3.71 us
    pallas_call x1, Pallas kernels, local(): pl.pallas_call(functools.partial(plan_kernel, slots, orbs, planes), out_s...  2.3 us
    pallas_call x1, Pallas kernels, run(): pl.pallas_call(functools.partial(sum_kernel, capacity, slots, lines, plan...  2.26 us
  transfers between devices with their start and end apart: 9, of which 7 were waited for; matrix products, arithmetic and copies ran while one was open for 0% of the time, Pallas kernels for 0%

profile of v1, /device:TPU:9, one launch (start us, length us, event | category | flops | bytes accessed | tf_op | source)
XLA Modules:
  0.0 110.0 jit_solution(6603255495244431877)
XLA Ops:
  0.7 1.2 %dynamic-slice = u32[1]{0:T(128)} dynamic-slice(u32[32]{0:T(128)} %constant.91, u32[]{:T(128)S(6)} %add.63), dynamic_slice_sizes={1} | dynamic-slice | bytes 12
  2.5 2.3 %plan.1 = (s32[147]{0:T(256)}, s32[144]{0:T(256)S(1)}) custom-call(s32[48]{0:T(128)} %own.1, s32[48]{0:T(128)} %step.1, s32[48]{0:T(128)} %remote.1, s32[1]{0:T(128)S(6)} %copy.40.count), custom_call_target="tpu_custom_call" | custom-call | tf_op jit(solution)/shard_map/plan/pallas_call | solution.py:226
  4.9 0.9 dynamic-update-slice
  5.8 8.9 %all-reduce = s32[1176]{0:T(1024)S(1)} all-reduce(s32[1176]{0:T(1024)S(1)} %dynamic-update-slice), channel_id=2, replica_groups=mesh['groups'=2,'blk'=4,'plane'=4] {'groups','blk'}, use_global_device_ids=true, to_apply=%add | all-reduce | flops 1176 | bytes 9408
  14.8 0.7 slice_reduce_fusion
  17.5 0.8 slice.13
  18.3 0.8 copy.33
  19.6 89.2 %conditional.1 = (f32[64,1,6400]{2,1,0:T(1,128)S(1)}) conditional(s32[]{:T(128)} %clamp.3, (f32[64,1,6400]{2,1,0:T(1,128)}, s32[3,48]{1,0:T(4,128)S(1)}, s32[144]{0:T(256)S(1)}, f32[160,160]{1,0:T(8,128)S(1)}, bf16[4,256,160]{2,1,0:T(8,128)(2,1)}, /*index=5*/bf16[4,256,160]{2,1,0:T(8,128)(2,1)}, ...), branch_computations={%region_1.2_spmd, %region_2.3_spmd, %region_3.4_spmd, %region_4.5_... | conditional | flops 25600 | bytes 34939500 | solution.py:316
  19.6 1.7 %pack.5 = (f32[1000,128]{1,0:T(8,128)S(1)}, f32[1000,128]{1,0:T(8,128)S(1)}, f32[1000,128]{1,0:T(8,128)S(1)}) custom-call(s32[3,48]{1,0:T(4,128)S(1)} %get-tuple-element.147.wanted, f32[3200,128]{1,0:T(8,128)} %bitcast.17), custom_call_target="tpu_custom_call" | custom-call | tf_op jit(solution)/shard_map/cond/branch_1_fun/pack/pallas_call | solution.py:262
  21.4 2.2 %collective-permute-start.10 = (f32[1000,128]{1,0:T(8,128)S(1)}, f32[1000,128]{1,0:T(8,128)S(1)}, u32[]{:S(2)}, u32[]{:S(2)}) collective-permute-start(f32[1000,128]{1,0:T(8,128)S(1)} %get-tuple-element.150), channel_id=1, source_target_pairs={{0,8},{4,12},{8,0},{12,4},{1,9},{5,13},{9,1},{13,5},{2,10},{6,14},... | collective-permute-start | bytes 1536008 | tf_op jit(solution)/shard_map/cond/branch_1_fun/ppermute | solution.py:271
  23.6 7.4 %collective-permute-done.9.refs_0_ = f32[1000,128]{1,0:T(8,128)S(1)} collective-permute-done((f32[1000,128]{1,0:T(8,128)S(1)}, f32[1000,128]{1,0:T(8,128)S(1)}, u32[]{:S(2)}, u32[]{:S(2)}) %collective-permute-start.9) | collective-permute-done | bytes 512032 | tf_op jit(solution)/shard_map/cond/branch_1_fun/ppermute | solution.py:271
  31.0 31.0 %collective-permute-done.10.refs_1_ = f32[1000,128]{1,0:T(8,128)S(1)} collective-permute-done((f32[1000,128]{1,0:T(8,128)S(1)}, f32[1000,128]{1,0:T(8,128)S(1)}, u32[]{:S(2)}, u32[]{:S(2)}) %collective-permute-start.10) | collective-permute-done | bytes 512032 | tf_op jit(solution)/shard_map/cond/branch_1_fun/ppermute | solution.py:271
  62.0 6.7 %collective-permute-done.11.refs_2_ = f32[1000,128]{1,0:T(8,128)S(1)} collective-permute-done((f32[1000,128]{1,0:T(8,128)S(1)}, f32[1000,128]{1,0:T(8,128)S(1)}, u32[]{:S(2)}, u32[]{:S(2)}) %collective-permute-start.11) | collective-permute-done | bytes 512032 | tf_op jit(solution)/shard_map/cond/branch_1_fun/ppermute | solution.py:271
  68.7 1.8 %density.5 = (f32[600,128]{1,0:T(8,128)S(1)}, f32[600,128]{1,0:T(8,128)S(1)}, f32[600,128]{1,0:T(8,128)S(1)}, f32[600,128]{1,0:T(8,128)S(1)}) custom-call(s32[144]{0:T(256)S(1)} %get-tuple-element.146.place, f32[3200,128]{1,0:T(8,128)S(1)} %bitcast.18, f32[1000,128]{1,0:T(8,128)S(1)} %collective-permute-done.9.refs_0_, ...), custom_call_target="tpu_custom_call" | custom-call | tf_op jit(solution)/shard_map/cond/branch_1_fun/density/pallas_call | solution.py:280
  71.1 1.2 %collective-permute-start.13 = (f32[600,128]{1,0:T(8,128)S(1)}, f32[600,128]{1,0:T(8,128)S(1)}, u32[]{:S(2)}, u32[]{:S(2)}) collective-permute-start(f32[600,128]{1,0:T(8,128)S(1)} %get-tuple-element.154), channel_id=1, source_target_pairs={{0,2},{1,3},{2,0},{3,1},{4,6},{5,7},{6,4},{7,5},{8,10},{9,11},{10,... | collective-permute-start | bytes 921608 | tf_op jit(solution)/shard_map/cond/branch_1_fun/ppermute | solution.py:208
  72.8 7.1 %collective-permute-done.13.refs_2_ = f32[600,128]{1,0:T(8,128)S(1)} collective-permute-done((f32[600,128]{1,0:T(8,128)S(1)}, f32[600,128]{1,0:T(8,128)S(1)}, u32[]{:S(2)}, u32[]{:S(2)}) %collective-permute-start.13) | collective-permute-done | bytes 307232 | tf_op jit(solution)/shard_map/cond/branch_1_fun/ppermute | solution.py:208
  79.9 6.7 %collective-permute-done.14.refs_3_ = f32[600,128]{1,0:T(8,128)S(1)} collective-permute-done((f32[600,128]{1,0:T(8,128)S(1)}, f32[600,128]{1,0:T(8,128)S(1)}, u32[]{:S(2)}, u32[]{:S(2)}) %collective-permute-start.14) | collective-permute-done | bytes 307232 | tf_op jit(solution)/shard_map/cond/branch_1_fun/ppermute | solution.py:208
  86.7 3.7 %transform.5 = (f32[600,128]{1,0:T(8,128)S(1)}, f32[600,128]{1,0:T(8,128)S(1)}, f32[600,128]{1,0:T(8,128)S(1)}, f32[600,128]{1,0:T(8,128)S(1)}) custom-call(f32[600,128]{1,0:T(8,128)S(1)} %get-tuple-element.152.refs_0_, f32[600,128]{1,0:T(8,128)S(1)} %collective-permute-done.12.refs_1_, f32[600,128]{1,0:T(8,128)S(1)} %collective-permute-done.13.refs_2_, ...), custom_call_target="tpu_custom_call" | custom-call | tf_op jit(solution)/shard_map/cond/branch_1_fun/transform/pallas_call | solution.py:290
  90.7 1.2 %collective-permute-start.16 = (f32[600,128]{1,0:T(8,128)S(1)}, f32[600,128]{1,0:T(8,128)S(1)}, u32[]{:S(2)}, u32[]{:S(2)}) collective-permute-start(f32[600,128]{1,0:T(8,128)S(1)} %get-tuple-element.167), channel_id=1, source_target_pairs={{0,2},{1,3},{2,0},{3,1},{4,6},{5,7},{6,4},{7,5},{8,10},{9,11},{10,... | collective-permute-start | bytes 921608 | tf_op jit(solution)/shard_map/cond/branch_1_fun/ppermute | solution.py:208
  91.9 0.7 collective-permute-start.17
  92.6 6.7 %collective-permute-done.16.refs_5_ = f32[600,128]{1,0:T(8,128)S(1)} collective-permute-done((f32[600,128]{1,0:T(8,128)S(1)}, f32[600,128]{1,0:T(8,128)S(1)}, u32[]{:S(2)}, u32[]{:S(2)}) %collective-permute-start.16) | collective-permute-done | bytes 307232 | tf_op jit(solution)/shard_map/cond/branch_1_fun/ppermute | solution.py:208
  99.3 7.0 %collective-permute-done.17.refs_6_ = f32[600,128]{1,0:T(8,128)S(1)} collective-permute-done((f32[600,128]{1,0:T(8,128)S(1)}, f32[600,128]{1,0:T(8,128)S(1)}, u32[]{:S(2)}, u32[]{:S(2)}) %collective-permute-start.17) | collective-permute-done | bytes 307232 | tf_op jit(solution)/shard_map/cond/branch_1_fun/ppermute | solution.py:208
  106.3 2.3 %sum.5 = f32[3200,128]{1,0:T(8,128)S(1)} custom-call(s32[144]{0:T(256)S(1)} %get-tuple-element.146.place, f32[1000,128]{1,0:T(8,128)S(1)} %collective-permute-done.9.refs_0_, f32[1000,128]{1,0:T(8,128)S(1)} %collective-permute-done.10.refs_1_, f32[1000,128]{1,0:T(8,128)S(1)} %collective-permute-done.11.refs_2_, f32[600,128]{1,0:T(8,128)S(1)} %get-tuple-element.165.refs_3_, ...), custom_call_target="tpu_custom_call" | custom-call | tf_op jit(solution)/shard_map/cond/branch_1_fun/sum/pallas_call | solution.py:304
  108.8 1.2 %copy-done.20 = f32[64,1,6400]{2,1,0:T(1,128)} copy-done((f32[64,1,6400]{2,1,0:T(1,128)}, f32[64,1,6400]{2,1,0:T(1,128)S(1)}, u32[]{:S(2)}) %copy-start.20) | copy-done | bytes 1638424
  (36 shorter events, 2.2 us)
Async XLA Ops:
  19.6 49.0 %copy-start.1 = (f32[64,1,6400]{2,1,0:T(1,128)S(1)}, f32[64,1,6400]{2,1,0:T(1,128)}, u32[]{:S(2)}) copy-start(f32[64,1,6400]{2,1,0:T(1,128)} %get-tuple-element.232) | copy-start | bytes 4915204 | tf_op jit(solution)/shard_map/cond
  21.3 9.7 %collective-permute-start.9 = (f32[1000,128]{1,0:T(8,128)S(1)}, f32[1000,128]{1,0:T(8,128)S(1)}, u32[]{:S(2)}, u32[]{:S(2)}) collective-permute-start(f32[1000,128]{1,0:T(8,128)S(1)} %get-tuple-element.149), channel_id=1, source_target_pairs={{0,4},{4,8},{8,12},{12,0},{1,5},{5,9},{9,13},{13,1},{2,6},{6,10},{... | collective-permute-start | bytes 1536008 | tf_op jit(solution)/shard_map/cond/branch_1_fun/ppermute | solution.py:271
  21.4 40.6 %collective-permute-start.10 = (f32[1000,128]{1,0:T(8,128)S(1)}, f32[1000,128]{1,0:T(8,128)S(1)}, u32[]{:S(2)}, u32[]{:S(2)}) collective-permute-start(f32[1000,128]{1,0:T(8,128)S(1)} %get-tuple-element.150), channel_id=1, source_target_pairs={{0,8},{4,12},{8,0},{12,4},{1,9},{5,13},{9,1},{13,5},{2,10},{6,14},... | collective-permute-start | bytes 1536008 | tf_op jit(solution)/shard_map/cond/branch_1_fun/ppermute | solution.py:271
  23.6 45.1 %collective-permute-start.11 = (f32[1000,128]{1,0:T(8,128)S(1)}, f32[1000,128]{1,0:T(8,128)S(1)}, u32[]{:S(2)}, u32[]{:S(2)}) collective-permute-start(f32[1000,128]{1,0:T(8,128)S(1)} %get-tuple-element.151), channel_id=1, source_target_pairs={{0,12},{4,0},{8,4},{12,8},{1,13},{5,1},{9,5},{13,9},{2,14},{6,2},{... | collective-permute-start | bytes 1536008 | tf_op jit(solution)/shard_map/cond/branch_1_fun/ppermute | solution.py:271
  68.6 18.0 %copy-start.5 = (bf16[4,256,160]{2,1,0:T(8,128)(2,1)S(1)}, bf16[4,256,160]{2,1,0:T(8,128)(2,1)}, u32[]{:S(2)}) copy-start(bf16[4,256,160]{2,1,0:T(8,128)(2,1)} %get-tuple-element.157.refs_5_) | copy-start | bytes 983044 | tf_op jit(solution)/shard_map/cond
  68.6 18.0 %copy-start.9 = (bf16[4,256,160]{2,1,0:T(8,128)(2,1)S(1)}, bf16[4,256,160]{2,1,0:T(8,128)(2,1)}, u32[]{:S(2)}) copy-start(bf16[4,256,160]{2,1,0:T(8,128)(2,1)} %get-tuple-element.156.refs_4_) | copy-start | bytes 983044 | tf_op jit(solution)/shard_map/cond
  68.6 18.0 %copy-start.13 = (bf16[4,160,256]{2,1,0:T(8,128)(2,1)S(1)}, bf16[4,160,256]{2,1,0:T(8,128)(2,1)}, u32[]{:S(2)}) copy-start(bf16[4,160,256]{2,1,0:T(8,128)(2,1)} %get-tuple-element.159.refs_7_) | copy-start | bytes 983044 | tf_op jit(solution)/shard_map/cond
  68.6 18.0 %copy-start.17 = (bf16[4,160,256]{2,1,0:T(8,128)(2,1)S(1)}, bf16[4,160,256]{2,1,0:T(8,128)(2,1)}, u32[]{:S(2)}) copy-start(bf16[4,160,256]{2,1,0:T(8,128)(2,1)} %get-tuple-element.158.refs_6_) | copy-start | bytes 983044 | tf_op jit(solution)/shard_map/cond
  68.7 18.0 %copy-start.22 = (bf16[160,160]{1,0:T(8,128)(2,1)S(1)}, bf16[160,160]{1,0:T(8,128)(2,1)}, u32[]{:S(2)}) copy-start(bf16[160,160]{1,0:T(8,128)(2,1)} %get-tuple-element.163.refs_11_) | copy-start | bytes 153604 | tf_op jit(solution)/shard_map/cond
  68.7 18.0 %copy-start.26 = (bf16[160,160]{1,0:T(8,128)(2,1)S(1)}, bf16[160,160]{1,0:T(8,128)(2,1)}, u32[]{:S(2)}) copy-start(bf16[160,160]{1,0:T(8,128)(2,1)} %get-tuple-element.162.refs_10_) | copy-start | bytes 153604 | tf_op jit(solution)/shard_map/cond
  68.7 18.0 %copy-start.30 = (bf16[160,160]{1,0:T(8,128)(2,1)S(1)}, bf16[160,160]{1,0:T(8,128)(2,1)}, u32[]{:S(2)}) copy-start(bf16[160,160]{1,0:T(8,128)(2,1)} %get-tuple-element.161.refs_9_) | copy-start | bytes 153604 | tf_op jit(solution)/shard_map/cond
  68.7 18.0 %copy-start.34 = (bf16[160,160]{1,0:T(8,128)(2,1)S(1)}, bf16[160,160]{1,0:T(8,128)(2,1)}, u32[]{:S(2)}) copy-start(bf16[160,160]{1,0:T(8,128)(2,1)} %get-tuple-element.160.refs_8_) | copy-start | bytes 153604 | tf_op jit(solution)/shard_map/cond
  70.5 2.3 %collective-permute-start.12 = (f32[600,128]{1,0:T(8,128)S(1)}, f32[600,128]{1,0:T(8,128)S(1)}, u32[]{:S(2)}, u32[]{:S(2)}) collective-permute-start(f32[600,128]{1,0:T(8,128)S(1)} %get-tuple-element.153), channel_id=1, source_target_pairs={{0,1},{1,0},{2,3},{3,2},{4,5},{5,4},{6,7},{7,6},{8,9},{9,8},{10,11... | collective-permute-start | bytes 921608 | tf_op jit(solution)/shard_map/cond/branch_1_fun/ppermute | solution.py:208
  71.1 8.9 %collective-permute-start.13 = (f32[600,128]{1,0:T(8,128)S(1)}, f32[600,128]{1,0:T(8,128)S(1)}, u32[]{:S(2)}, u32[]{:S(2)}) collective-permute-start(f32[600,128]{1,0:T(8,128)S(1)} %get-tuple-element.154), channel_id=1, source_target_pairs={{0,2},{1,3},{2,0},{3,1},{4,6},{5,7},{6,4},{7,5},{8,10},{9,11},{10,... | collective-permute-start | bytes 921608 | tf_op jit(solution)/shard_map/cond/branch_1_fun/ppermute | solution.py:208
  72.3 14.4 %collective-permute-start.14 = (f32[600,128]{1,0:T(8,128)S(1)}, f32[600,128]{1,0:T(8,128)S(1)}, u32[]{:S(2)}, u32[]{:S(2)}) collective-permute-start(f32[600,128]{1,0:T(8,128)S(1)} %get-tuple-element.155), channel_id=1, source_target_pairs={{0,3},{1,2},{2,1},{3,0},{4,7},{5,6},{6,5},{7,4},{8,11},{9,10},{10,... | collective-permute-start | bytes 921608 | tf_op jit(solution)/shard_map/cond/branch_1_fun/ppermute | solution.py:208
  90.4 2.2 %collective-permute-start.15 = (f32[600,128]{1,0:T(8,128)S(1)}, f32[600,128]{1,0:T(8,128)S(1)}, u32[]{:S(2)}, u32[]{:S(2)}) collective-permute-start(f32[600,128]{1,0:T(8,128)S(1)} %get-tuple-element.166), channel_id=1, source_target_pairs={{0,1},{1,0},{2,3},{3,2},{4,5},{5,4},{6,7},{7,6},{8,9},{9,8},{10,11... | collective-permute-start | bytes 921608 | tf_op jit(solution)/shard_map/cond/branch_1_fun/ppermute | solution.py:208
  90.7 8.6 %collective-permute-start.16 = (f32[600,128]{1,0:T(8,128)S(1)}, f32[600,128]{1,0:T(8,128)S(1)}, u32[]{:S(2)}, u32[]{:S(2)}) collective-permute-start(f32[600,128]{1,0:T(8,128)S(1)} %get-tuple-element.167), channel_id=1, source_target_pairs={{0,2},{1,3},{2,0},{3,1},{4,6},{5,7},{6,4},{7,5},{8,10},{9,11},{10,... | collective-permute-start | bytes 921608 | tf_op jit(solution)/shard_map/cond/branch_1_fun/ppermute | solution.py:208
  91.9 14.4 %collective-permute-start.17 = (f32[600,128]{1,0:T(8,128)S(1)}, f32[600,128]{1,0:T(8,128)S(1)}, u32[]{:S(2)}, u32[]{:S(2)}) collective-permute-start(f32[600,128]{1,0:T(8,128)S(1)} %get-tuple-element.168), channel_id=1, source_target_pairs={{0,3},{1,2},{2,1},{3,0},{4,7},{5,6},{6,5},{7,4},{8,11},{9,10},{10,... | collective-permute-start | bytes 921608 | tf_op jit(solution)/shard_map/cond/branch_1_fun/ppermute | solution.py:208
  108.8 1.2 %copy-start.20 = (f32[64,1,6400]{2,1,0:T(1,128)}, f32[64,1,6400]{2,1,0:T(1,128)S(1)}, u32[]{:S(2)}) copy-start(f32[64,1,6400]{2,1,0:T(1,128)S(1)} %get-tuple-element.348) | copy-start | bytes 4915204
